TPU v7x, 32 devices: a whole 2x2x4 slice. The times are simulated.
32 devices in a mesh: rep: 2 (over y), serve: 4 (over x, core), tp: 4 (over z).
Axes of the slice: x: 2, y: 2, z: 4, core: 2. Of those that a mesh axis runs over, the one named last changes fastest.
Arguments:
- hidden: bfloat16 [3072, 8192], P(('rep', 'serve', 'tp')), parts along dimension 0, may hold values from -6 to 6
- kv_weight: bfloat16 [8192, 2048], P('tp'), may hold values from -0.0625 to 0.0625
- a_store: bfloat16 [128, 8192, 64], P('serve', 'tp'), may hold values from -0.0625 to 0.0625
- b_store: bfloat16 [128, 64, 2048], P('serve', None, 'tp'), may hold values from -0.75 to 0.75
- home: int32 [256], P('rep'), parts along dimension 0, may hold values from 0 to 127, as said below
- wanted: int32 [8, 16], P('rep'), parts along dimension 0, may hold values from 0 to 127, as said below
- tile_slot: int32 [192], P(('rep', 'serve')), parts along dimension 0, may hold values from 0 to 15, as said below
Outputs:
- kv_out: bfloat16 [3072, 2048], P(('rep', 'serve'), 'tp'), parts along dimension 0
There are 2 independent parts, one for each index of `rep`. A program takes and returns all parts, laid end to end along the dimension named above; an argument that names none is the same for every part. Nothing has to cross between parts.
Inputs may be any that keep to these rules, and one draw needn't show every extreme that they name: home is a permutation: adapter a sits in store row home[a]; store rows s * 32 to (s + 1) * 32 - 1 lie on serve index s. `wanted`: each group's 16 entries are distinct adapters; at most 4 of one group's entries sit on one serve index, and in every group exactly 4 sit on some serve index. `tile_slot`: the tiles of group g are tiles g * 24 to (g + 1) * 24 - 1; their entries never fall along the group, and every entry of the group's list is used by one tile or more.
All inputs are finite; a program needn't handle non-finite values.
Results may differ from a plain program's by a relative error of at most 0.001.
Values may be sent and summed in bfloat16 or wider, within the bound.
A program may use at most 128 MiB of HBM per device.

v0:
```python
import jax
import jax.numpy as jnp
from jax import lax
from jax.sharding import PartitionSpec as P

adapter_scale = 0.5


def entry_routes(home, wanted, held_count, groups):
    store_rows = jnp.take(home, wanted, axis=0)
    owner_index = store_rows // held_count
    local_slot = store_rows % held_count
    owners = lax.broadcasted_iota(jnp.int32, (1, 1, groups), 2)
    same_store = (owner_index[:, :, None] == owners).astype(jnp.int32)
    earlier = jnp.cumsum(same_store, axis=1) - same_store
    slot_rank = jnp.sum(earlier * same_store, axis=2)
    return (owner_index, local_slot, slot_rank)


def body(hidden, kv_weight, a_store, b_store, home, wanted, tile_slot):
    groups = lax.axis_size("serve")
    my_group = lax.axis_index("serve")
    held_count = a_store.shape[0]
    rank_width = a_store.shape[2]
    slot_count = max(2, (wanted.shape[1] + groups - 1) // groups)
    slices = lax.all_to_all(hidden, "tp", split_axis=1, concat_axis=0, tiled=True)
    decode_row_count = slices.shape[0]
    tile_count = tile_slot.shape[0]
    tile_rows = decode_row_count // tile_count
    owner_index, local_slot, slot_rank = entry_routes(home, wanted, held_count, groups)
    slot_ids = lax.broadcasted_iota(jnp.int32, (1, slot_count, 1), 1)
    matches = (owner_index[:, None, :] == my_group) & (slot_rank[:, None, :] == slot_ids)
    picked = jnp.sum(jnp.where(matches, local_slot[:, None, :], 0), axis=2).reshape(-1)
    send_shrink = jnp.take(a_store, picked, axis=0).reshape(
        (groups, slot_count) + a_store.shape[1:]
    )
    send_expand = jnp.take(b_store, picked, axis=0).reshape(
        (groups, slot_count) + b_store.shape[1:]
    )
    got_shrink, got_expand = (
        lax.all_to_all(send_shrink, "serve", split_axis=0, concat_axis=0, tiled=True),
        lax.all_to_all(send_expand, "serve", split_axis=0, concat_axis=0, tiled=True),
    )
    local_entries = jnp.take(owner_index, my_group, axis=0) * slot_count + jnp.take(
        slot_rank, my_group, axis=0
    )
    shrink_panels = jnp.take(
        got_shrink.reshape((groups * slot_count,) + a_store.shape[1:]), local_entries, axis=0
    )
    expand_panels = jnp.take(
        got_expand.reshape((groups * slot_count,) + b_store.shape[1:]), local_entries, axis=0
    )
    base_part = jnp.dot(slices, kv_weight, preferred_element_type=jnp.float32)
    tile_shrink = jnp.take(shrink_panels, tile_slot, axis=0)
    tiled_rows = slices.reshape(tile_count, tile_rows, slices.shape[1])
    low_part = jnp.einsum(
        "tkd,tdr->tkr", tiled_rows, tile_shrink, preferred_element_type=jnp.float32
    )
    low_part = low_part.reshape(decode_row_count, rank_width)
    base_output = lax.psum_scatter(base_part, "tp", scatter_dimension=1, tiled=True)
    lowrank = lax.psum(low_part, "tp")
    tile_expand = jnp.take(expand_panels, tile_slot, axis=0).astype(jnp.float32)
    adapter_update = jnp.einsum(
        "tkr,trc->tkc",
        lowrank.reshape(tile_count, tile_rows, rank_width),
        tile_expand,
        precision=lax.Precision.HIGHEST,
        preferred_element_type=jnp.float32,
    )
    return (base_output + adapter_scale * adapter_update.reshape(decode_row_count, -1)).astype(
        jnp.bfloat16
    )


def solution(mesh):
    in_specs = (
        P(("rep", "serve", "tp"), None),
        P("tp", None),
        P("serve", "tp", None),
        P("serve", None, "tp"),
        P("rep"),
        P("rep", None),
        P(("rep", "serve")),
    )
    out_specs = P(("rep", "serve"), "tp")
    return jax.shard_map(body, mesh=mesh, in_specs=in_specs, out_specs=out_specs, check_vma=False)
```

profile of v0, /device:TPU:0, one launch (start us, length us, event | category | flops | bytes accessed | tf_op | source)
XLA Modules:
  0.0 228.2 jit_solution(2337234678101123225)
XLA Ops:
  6.5 0.0 copy-start
  6.5 0.8 compare_select_fusion.1
  7.4 0.1 reshape.189
  7.5 1.4 gather_fusion
  8.9 0.1 reshape.188
  9.0 0.7 add_select_fusion
  9.7 0.7 broadcast_compare_fusion
  10.4 0.1 fusion.15
  10.5 0.2 select_reduce_fusion
  10.7 0.2 select_reduce_fusion.1
  10.9 0.1 reshape.137
  11.0 6.1 %gather_fusion.1 = bf16[16,2048,64]{1,2,0:T(8,128)(2,1)} fusion(bf16[32,2048,64]{1,2,0:T(8,128)(2,1)} %param.11, s32[1024]{0:T(1024)S(1)} %pad_clamp_fusion.2), kind=kCustom, calls=%fused_computation.1 | custom fusion | bytes 8388672 | tf_op jit(solution)/shard_map/jit(_take)/gather | solution.py:34
  17.1 4.6 %broadcast_select_fusion.1 = bf16[4,4,2048,64]{2,3,1,0:T(8,128)(2,1)} fusion(bf16[4,4,2048,64]{2,3,1,0:T(8,128)(2,1)} %bitcast.41, pred[4,4]{1,0:T(4,128)(4,1)S(1)} %compare_and_fusion), kind=kLoop, calls=%fused_computation.11 | loop fusion | flops 2097152 | bytes 8388624 | tf_op jit(solution)/shard_map/jit(_take)/select_n | solution.py:34
  21.7 4.9 %all-to-all-start.1 = ((bf16[4,4,2048,64]{2,3,1,0:T(8,128)(2,1)}), bf16[4,4,2048,64]{2,3,1,0:T(8,128)(2,1)}, u32[]{:S(2)}, u32[]{:S(2)}) async-start(bf16[4,4,2048,64]{2,3,1,0:T(8,128)(2,1)} %broadcast_select_fusion.1), calls=%async_computation.2 | async-start | bytes 8388608 | tf_op jit(solution)/shard_map/all_to_all | solution.py:41
  26.6 0.0 copy-start.1
  26.6 2.8 %copy.14 = bf16[12,4,8,2048]{3,2,0,1:T(8,128)(2,1)} copy(bf16[12,4,8,2048]{3,2,1,0:T(8,128)(2,1)} %bitcast.45) | data formatting | bytes 3145728 | tf_op jit(solution)/shard_map/all_to_all | solution.py:26
  29.4 46.0 %all-to-all-done.1 = bf16[4,4,2048,64]{2,3,1,0:T(8,128)(2,1)} async-done(((bf16[4,4,2048,64]{2,3,1,0:T(8,128)(2,1)}), bf16[4,4,2048,64]{2,3,1,0:T(8,128)(2,1)}, u32[]{:S(2)}, u32[]{:S(2)}) %all-to-all-start.1) | async-done | bytes 4194336 | tf_op jit(solution)/shard_map/all_to_all | solution.py:41
  75.4 5.7 %all-to-all-start = ((bf16[96,4,2048]{2,0,1:T(8,128)(2,1)}), bf16[96,4,2048]{2,0,1:T(8,128)(2,1)}, u32[]{:S(2)}, u32[]{:S(2)}) async-start(bf16[96,4,2048]{2,0,1:T(8,128)(2,1)} %bitcast.42), calls=%async_computation | async-start | bytes 3145728 | tf_op jit(solution)/shard_map/all_to_all | solution.py:26
  81.2 0.0 all-reduce.2.cloned.1.call-start
  81.2 0.0 copy-done.1
  81.2 5.0 %gather_fusion.2 = bf16[16,2048,64]{1,2,0:T(8,128)(2,1)} fusion(bf16[16,2048,64]{1,2,0:T(8,128)(2,1)} %bitcast.6, s32[1024]{0:T(1024)S(1)} %pad_clamp_fusion.1), kind=kCustom, calls=%fused_computation.2 | custom fusion | bytes 8388672 | tf_op jit(solution)/shard_map/jit(_take)/gather | solution.py:47
  86.3 4.7 %broadcast_select_fusion = bf16[16,2048,64]{1,2,0:T(8,128)(2,1)} fusion(bf16[16,2048,64]{1,2,0:T(8,128)(2,1)} %gather_fusion.2, pred[16]{0:T(512)(128)(4,1)S(1)} %get-tuple-element.17), kind=kLoop, calls=%fused_computation.10 | loop fusion | flops 2097152 | bytes 8388624 | tf_op jit(solution)/shard_map/jit(_take)/select_n | solution.py:47
  91.0 6.6 %gather_fusion.3 = bf16[24,2048,64]{1,2,0:T(8,128)(2,1)} fusion(bf16[16,2048,64]{1,2,0:T(8,128)(2,1)} %broadcast_select_fusion, s32[1024]{0:T(1024)S(1)} %pad_clamp_fusion), kind=kCustom, calls=%fused_computation.3 | custom fusion | bytes 12583008 | tf_op jit(solution)/shard_map/jit(_take)/gather | solution.py:54
  97.6 20.4 %all-to-all-done = bf16[96,4,2048]{2,0,1:T(8,128)(2,1)} async-done(((bf16[96,4,2048]{2,0,1:T(8,128)(2,1)}), bf16[96,4,2048]{2,0,1:T(8,128)(2,1)}, u32[]{:S(2)}, u32[]{:S(2)}) %all-to-all-start) | async-done | bytes 1572896 | tf_op jit(solution)/shard_map/all_to_all | solution.py:26
  118.0 5.7 %fusion.10 = f32[24,16,64]{2,1,0:T(8,128)} fusion(bf16[24,16,2048]{2,1,0:T(8,128)(2,1)} %bitcast.7, bf16[24,2048,64]{1,2,0:T(8,128)(2,1)} %gather_fusion.3, pred[24]{0:T(512)(128)(4,1)S(1)} %compare_and_fusion.2), kind=kOutput, calls=%fused_computation.18 | convolution fusion | flops 103809024 | bytes 7962648 | tf_op jit(solution)/shard_map/tkd,tdr->tkr/dot_general | solution.py:56
  123.8 0.0 all-reduce.2.cloned.1.call-update
  123.8 0.0 reduce-scatter.2.cloned.1.call-start
  123.8 9.0 %fusion.25 = f32[384,2048]{1,0:T(8,128)} fusion(bf16[384,2048]{1,0:T(8,128)(2,1)} %bitcast.1, bf16[2048,2048]{1,0:T(8,128)(2,1)} %param.10), kind=kOutput, calls=%fused_computation.61 | convolution fusion | flops 3221225472 | bytes 13107200 | tf_op jit(solution)/shard_map/dot_general | solution.py:53
  132.8 0.0 reduce-scatter.2.cloned.1.call-update
  132.8 0.0 copy-done
  132.8 0.6 gather_fusion.4
  133.4 0.2 broadcast_select_fusion.3
  133.6 16.9 %all_to_all.29 = bf16[4,4,64,512]{3,2,1,0:T(8,128)(2,1)S(1)} all-to-all(bf16[4,4,64,512]{3,2,1,0:T(8,128)(2,1)S(1)} %broadcast_select_fusion.3), channel_id=1, replica_groups=mesh['rep'=2,'serve'=4,'tp'=4] {'serve'}, dimensions={0} | all-to-all | bytes 2097152 | tf_op jit(solution)/shard_map/all_to_all | solution.py:42
  150.5 1.6 gather_fusion.5
  152.1 1.4 broadcast_select_fusion.2
  153.5 1.8 gather_fusion.6
  155.3 1.7 all-reduce.2.cloned.1.call-done
  157.0 2.3 %fusion.7 = f32[24,16,512]{2,1,0:T(8,128)S(1)} fusion(f32[24,16,64]{2,1,0:T(8,128)} %all-reduce.2.cloned.1.call-done, bf16[24,64,512]{2,1,0:T(8,128)(2,1)} %gather_fusion.6, pred[24]{0:T(512)(128)(4,1)S(1)} %compare_and_fusion.2), kind=kOutput, calls=%fused_computation.17 | convolution fusion | flops 151977984 | bytes 2457624 | tf_op jit(solution)/shard_map/tkr,trc->tkc/dot_general | solution.py:63
  159.4 60.1 %reduce-scatter.2.cloned.1.call-done = f32[384,512]{1,0:T(8,128)} async-done(((f32[384,2048]{1,0:T(8,128)}), f32[384,512]{1,0:T(8,128)}) %reduce-scatter.2.cloned.1.call-update) | async-done | bytes 786448 | tf_op jit(solution)/shard_map/reduce_scatter | solution.py:60
  219.4 2.0 fusion.13
  (10 shorter events, 0.1 us)
Async XLA Ops:
  6.5 126.3 %copy-start = (bf16[32,64,512]{2,1,0:T(8,128)(2,1)S(1)}, bf16[32,64,512]{2,1,0:T(8,128)(2,1)}, u32[]{:S(2)}) copy-start(bf16[32,64,512]{2,1,0:T(8,128)(2,1)} %param.12) | copy-start | bytes 6291460
  21.7 53.7 %all-to-all-start.1 = ((bf16[4,4,2048,64]{2,3,1,0:T(8,128)(2,1)}), bf16[4,4,2048,64]{2,3,1,0:T(8,128)(2,1)}, u32[]{:S(2)}, u32[]{:S(2)}) async-start(bf16[4,4,2048,64]{2,3,1,0:T(8,128)(2,1)} %broadcast_select_fusion.1), calls=%async_computation.2 | async-start | bytes 8388608 | tf_op jit(solution)/shard_map/all_to_all | solution.py:41
  26.6 54.6 %copy-start.1 = (s32[24]{0:T(128)S(1)}, s32[24]{0:T(128)}, u32[]{:S(2)}) copy-start(s32[24]{0:T(128)} %param.15) | copy-start | bytes 292
  75.4 42.6 %all-to-all-start = ((bf16[96,4,2048]{2,0,1:T(8,128)(2,1)}), bf16[96,4,2048]{2,0,1:T(8,128)(2,1)}, u32[]{:S(2)}, u32[]{:S(2)}) async-start(bf16[96,4,2048]{2,0,1:T(8,128)(2,1)} %bitcast.42), calls=%async_computation | async-start | bytes 3145728 | tf_op jit(solution)/shard_map/all_to_all | solution.py:26
  81.2 75.9 %all-reduce.2.cloned.1.call-start = ((), (), s32[]{:S(2)}) async-start(), calls=%async_computation.5 | async-start | bytes 393216 | tf_op jit(solution)/shard_map/psum | solution.py:61
  123.8 95.7 %reduce-scatter.2.cloned.1.call-start = ((), (), s32[]{:S(2)}) async-start(), calls=%async_computation.4 | async-start | bytes 3932160 | tf_op jit(solution)/shard_map/reduce_scatter | solution.py:60
Sparse Core Ops, SparseCore 0:
  123.9 33.0 all-reduce.1
  159.4 59.9 reduce-scatter.1
where the time goes:
time: 229 us; the launch traced here: 228 us
  waiting for transfers between devices  128 us (56%)
  local copies, waits for them, and re-layouts  26.4 us (12%)
  matrix products  17 us (7%)
  blocking collectives  16.9 us (7%)
  other arithmetic  15.6 us (7%)
  between operations  13.5 us (6%)
  starting transfers between devices  10.6 us (5%)
    reduce_scatter x1, waiting for transfers between devices, body(): lax.psum_scatter(base_part, 'tp', scatter_dimension=1, tiled=True)  60.1 us
    all_to_all x1, waiting for transfers between devices, body(): lax.all_to_all(send_shrink, 'serve', split_axis=0, concat_axis=0, tiled=T...  46 us
    all_to_all x1, waiting for transfers between devices, body(): lax.all_to_all(hidden, 'tp', split_axis=1, concat_axis=0, tiled=True)  20.4 us
    all_to_all x1, blocking collectives, body(): lax.all_to_all(send_expand, 'serve', split_axis=0, concat_axis=0, tiled=T...  16.9 us
    dot_general x1, matrix products, body(): base_part = jnp.dot(slices, kv_weight, preferred_element_type=jnp.float32)  8.96 us
    gather x1, local copies, waits for them, and re-layouts, body(): tile_shrink = jnp.take(shrink_panels, tile_slot, axis=0)  6.64 us
    gather x1, local copies, waits for them, and re-layouts, body(): jnp.take(a_store, picked, axis=0)  6.12 us
    dot_general x1, matrix products, body(): jnp.einsum('tkd,tdr->tkr', tiled_rows, tile_shrink, preferred_element_typ...  5.72 us
  transfers between devices with their start and end apart: 4, of which 4 were waited for; matrix products, arithmetic and copies ran while one was open for 16% of the time, Pallas kernels for 0%

commit v1 on v0

v1 whole, which is shorter than its diff:
```python
import functools

import jax
import jax.numpy as jnp
from jax import lax
from jax.experimental import pallas as pl
from jax.experimental.pallas import tpu as pltpu
from jax.sharding import PartitionSpec as P

adapter_scale = 0.5
LEVELS = 32767.0


def flip(index, step, count):
    result, bit = 0, 1
    while bit < count:
        on = lax.rem(lax.div(index, jnp.int32(bit)), jnp.int32(2))
        if isinstance(step, int):
            turned = 1 - on if step & bit else on
        else:
            turned = lax.rem(on + lax.rem(lax.div(step, jnp.int32(bit)), jnp.int32(2)), jnp.int32(2))
        result = result + bit * turned
        bit *= 2
    return result


def quantize(values):
    top = jnp.maximum(jnp.max(jnp.abs(values)), 1e-30)
    coded = jnp.round(values * (LEVELS / top)).astype(jnp.int32).astype(jnp.int16)
    return coded, jnp.full((8, 128), top * (1.0 / LEVELS), jnp.float32)


def restore(coded, scale):
    return coded.astype(jnp.int32).astype(jnp.float32) * scale


def kernel(
    cfg,
    home, wanted, tile_slot, hidden, weight, a_store, b_store,
    out,
    xs, w_vm, a_vm, b_vm, send_a, send_b, got_a, got_b,
    p_send, p_scale_send, p_recv, p_scale_recv,
    l_send, l_scale_send, l_recv, l_scale_recv,
    own, row_slot, low_rows, picks, places,
    local_sem, x_send, x_recv, a_send, a_recv, bs_send, bs_recv,
    ps_send, ps_recv, psc_send, psc_recv,
    ls_send, ls_recv, lsc_send, lsc_recv,
):
    n_tp, n_serve, cap, held = cfg
    need = wanted.shape[1]
    tiles = tile_slot.shape[0]
    block, depth = xs.shape[1], xs.shape[2]
    rows = n_tp * block
    tile_rows = rows // tiles
    rank = a_vm.shape[1]
    feats = out.shape[1]
    half = rows // 2
    me = lax.axis_index("tp")
    group = lax.axis_index("serve")

    def x_copy(u):
        j = flip(me, u, n_tp)
        return pltpu.make_async_remote_copy(
            src_ref=hidden.at[:, pl.ds(pl.multiple_of(j * depth, depth), depth)],
            dst_ref=xs.at[u],
            send_sem=x_send.at[u], recv_sem=x_recv.at[u],
            device_id={"tp": j},
        )

    def panel_copy(src, dst, ssem, rsem, u, landing):
        d = flip(group, u, n_serve)
        return pltpu.make_async_remote_copy(
            src_ref=src.at[u], dst_ref=dst.at[landing],
            send_sem=ssem.at[u], recv_sem=rsem.at[u],
            device_id={"serve": d},
        )

    def part_copies(u, t):
        c = flip(me, u, n_tp)
        return (
            pltpu.make_async_remote_copy(
                src_ref=p_send.at[u, t], dst_ref=p_recv.at[u, t],
                send_sem=ps_send.at[u, t], recv_sem=ps_recv.at[u, t],
                device_id={"tp": c},
            ),
            pltpu.make_async_remote_copy(
                src_ref=p_scale_send.at[u, t], dst_ref=p_scale_recv.at[u, t],
                send_sem=psc_send.at[u, t], recv_sem=psc_recv.at[u, t],
                device_id={"tp": c},
            ),
        )

    def low_copies(u):
        c = flip(me, u, n_tp)
        return (
            pltpu.make_async_remote_copy(
                src_ref=l_send, dst_ref=l_recv.at[u],
                send_sem=ls_send.at[u], recv_sem=ls_recv.at[u],
                device_id={"tp": c},
            ),
            pltpu.make_async_remote_copy(
                src_ref=l_scale_send, dst_ref=l_scale_recv.at[u],
                send_sem=lsc_send.at[u], recv_sem=lsc_recv.at[u],
                device_id={"tp": c},
            ),
        )

    load_a = pltpu.make_async_copy(a_store, a_vm, local_sem.at[0])
    load_b = pltpu.make_async_copy(b_store, b_vm, local_sem.at[1])
    load_x = pltpu.make_async_copy(
        hidden.at[:, pl.ds(pl.multiple_of(me * depth, depth), depth)], xs.at[0], local_sem.at[2]
    )
    load_w = pltpu.make_async_copy(weight, w_vm, local_sem.at[3])
    load_a.start()
    load_x.start()
    load_b.start()
    load_w.start()

    barrier = pltpu.get_barrier_semaphore()
    for u in range(1, n_tp):
        pl.semaphore_signal(barrier, inc=1, device_id={"tp": flip(me, u, n_tp)})
    for u in range(1, n_serve):
        pl.semaphore_signal(barrier, inc=1, device_id={"serve": flip(group, u, n_serve)})
    pl.semaphore_wait(barrier, n_tp - 1 + n_serve - 1)

    for u in range(1, n_tp):
        x_copy(u).start()

    @pl.loop(0, n_serve)
    def _(u):
        d = flip(group, u, n_serve)

        def step(e, carry):
            count, chosen = carry[0], list(carry[1:])
            row = home[wanted[d, e]]
            hit = (row // held) == group
            slot = row % held
            for i in range(cap):
                chosen[i] = jnp.where(jnp.logical_and(hit, count == i), slot, chosen[i])
            return (count + jnp.where(hit, 1, 0), *chosen)

        result = lax.fori_loop(0, need, step, tuple(jnp.int32(0) for _ in range(cap + 1)))
        for i in range(cap):
            picks[u, i] = result[1 + i]

    load_a.wait()

    for u in range(n_serve - 1, 0, -1):
        for i in range(cap):
            send_a[u, i * rank:(i + 1) * rank, :] = a_vm[picks[u, i]]
        panel_copy(send_a, got_a, a_send, a_recv, u, u).start()

    load_b.wait()

    for u in range(n_serve - 1, 0, -1):
        for i in range(cap):
            send_b[u, i * rank:(i + 1) * rank, :] = b_vm[picks[u, i]]
        panel_copy(send_b, got_b, bs_send, bs_recv, u, u).start()

    for i in range(cap):
        send_a[0, i * rank:(i + 1) * rank, :] = a_vm[picks[0, i]]
        send_b[0, i * rank:(i + 1) * rank, :] = b_vm[picks[0, i]]

    @pl.loop(0, need)
    def _(e):
        owner = home[wanted[group, e]] // held

        def step(f, count):
            same = (home[wanted[group, f]] // held) == owner
            return count + jnp.where(jnp.logical_and(same, f < e), 1, 0)

        earlier = lax.fori_loop(0, need, step, jnp.int32(0))
        places[e] = flip(owner, group, n_serve) * cap + earlier

    per_block = tiles // n_tp
    for t in range(n_tp):
        j = flip(me, t, n_tp)

        @pl.loop(0, per_block)
        def _(k):
            place = places[tile_slot[j * per_block + k]]
            row_slot[t, pl.ds(pl.multiple_of(k * tile_rows, tile_rows), tile_rows), :] = jnp.full(
                (tile_rows, 128), place, jnp.int32
            )

    load_x.wait()
    load_w.wait()

    for t in range(n_tp):
        j = flip(me, t, n_tp)
        if t:
            x_copy(t).wait_recv()
        for u in range(1, n_tp):
            c = flip(me, u, n_tp)
            part = jnp.dot(
                xs[t], w_vm[:, pl.ds(pl.multiple_of(c * feats, feats), feats)],
                preferred_element_type=jnp.float32,
            )
            coded, scale = quantize(part)
            p_send[u, t] = coded
            p_scale_send[u, t] = scale
            for copy in part_copies(u, t):
                copy.start()

        own[t] = jnp.dot(
            xs[t], w_vm[:, pl.ds(pl.multiple_of(me * feats, feats), feats)],
            preferred_element_type=jnp.float32,
        )

    lane = lax.broadcasted_iota(jnp.int32, (rows, 128), 1)
    lane_half = lane // rank
    slots = row_slot[...].reshape(rows, 128)
    per = 128 // rank
    l_sum = jnp.zeros((rows, 128), jnp.float32)
    for u in range(n_serve):
        if u > 0:
            panel_copy(send_a, got_a, a_send, a_recv, u, u).wait_recv()
        found = lax.dot_general(
            xs[...].reshape(rows, depth), (got_a[u] if u else send_a[0]), (((1,), (1,)), ((), ())),
            preferred_element_type=jnp.float32,
        )
        for h in range(cap // per):
            keep = slots == u * cap + h * per + lane_half
            l_sum = l_sum + jnp.where(keep, found[:, h * 128:(h + 1) * 128], 0.0)
    l_sum = l_sum + pltpu.roll(l_sum, rank, 1)
    for t in range(n_tp):
        low_rows[flip(me, t, n_tp)] = l_sum[t * block:(t + 1) * block]
    l_sum = low_rows[...].reshape(rows, 128)
    left = lax.broadcasted_iota(jnp.int32, (half, 128), 1) < rank
    packed = jnp.where(left, l_sum[:half], l_sum[half:])
    coded, scale = quantize(packed)
    l_send[...] = coded
    l_scale_send[...] = scale
    for u in range(1, n_tp):
        for copy in low_copies(u):
            copy.start()
    total = packed
    for u in range(1, n_tp):
        for copy in low_copies(u):
            copy.wait_recv()
        total = total + restore(l_recv[u], l_scale_recv[u][0:1, :])
    turned = pltpu.roll(total, rank, 1)
    low_rows[...] = jnp.concatenate(
        [jnp.where(left, total, turned), jnp.where(left, turned, total)], axis=0
    ).reshape(n_tp, block, 128)
    low = jnp.concatenate([low_rows[flip(me, t, n_tp)] for t in range(n_tp)], axis=0)

    high = low.astype(jnp.bfloat16).astype(jnp.float32)
    rest = low - high
    update = jnp.zeros((rows, feats), jnp.float32)
    for u in range(n_serve):
        if u > 0:
            panel_copy(send_b, got_b, bs_send, bs_recv, u, u).wait_recv()
        for h in range(cap // per):
            keep = slots == u * cap + h * per + lane_half
            panel = (got_b if u else send_b)[u, h * 128:(h + 1) * 128, :]
            for piece in (high, rest):
                update = update + jnp.dot(
                    jnp.where(keep, piece, 0.0).astype(jnp.bfloat16), panel,
                    preferred_element_type=jnp.float32,
                )
    own[...] = own[...] + adapter_scale * update.reshape(n_tp, block, feats)

    for t in range(n_tp):
        j = flip(me, t, n_tp)
        result = own[t]
        for u in range(1, n_tp):
            for copy in part_copies(u, u ^ t):
                copy.wait_recv()
            result = result + restore(p_recv[u, u ^ t], p_scale_recv[u, u ^ t, 0:1, 0:1])
        out[pl.ds(pl.multiple_of(j * block, block), block), :] = result.astype(jnp.bfloat16)

    for u in range(1, n_tp):
        x_copy(u).wait_send()
        for copy in low_copies(u):
            copy.wait_send()

        for t in range(n_tp):
            for copy in part_copies(u, t):
                copy.wait_send()

    for u in range(1, n_serve):
        panel_copy(send_a, got_a, a_send, a_recv, u, u).wait_send()
        panel_copy(send_b, got_b, bs_send, bs_recv, u, u).wait_send()


def body(hidden, kv_weight, a_store, b_store, home, wanted, tile_slot):
    n_tp = lax.axis_size("tp")
    n_serve = lax.axis_size("serve")
    block, width = hidden.shape
    depth = width // n_tp
    held, _, rank = a_store.shape
    feats = b_store.shape[2]
    rows = block * n_tp
    cap = max(2, (wanted.shape[1] + n_serve - 1) // n_serve)
    cap = cap + cap % 2
    panels = jnp.transpose(a_store, (0, 2, 1))
    bf16, f32, i16 = jnp.bfloat16, jnp.float32, jnp.int16
    dma = pltpu.SemaphoreType.DMA
    smem = pl.BlockSpec(memory_space=pltpu.SMEM)
    hbm = pl.BlockSpec(memory_space=pl.ANY)
    scratch = [
        pltpu.VMEM((n_tp, block, depth), bf16),
        pltpu.VMEM(kv_weight.shape, bf16),
        pltpu.VMEM(panels.shape, bf16),
        pltpu.VMEM(b_store.shape, bf16),
        pltpu.VMEM((n_serve, cap * rank, depth), bf16),
        pltpu.VMEM((n_serve, cap * rank, feats), bf16),
        pltpu.VMEM((n_serve, cap * rank, depth), bf16),
        pltpu.VMEM((n_serve, cap * rank, feats), bf16),
        pltpu.VMEM((n_tp, n_tp, block, feats), i16),
        pltpu.VMEM((n_tp, n_tp, 8, 128), f32),
        pltpu.VMEM((n_tp, n_tp, block, feats), i16),
        pltpu.VMEM((n_tp, n_tp, 8, 128), f32),
        pltpu.VMEM((rows // 2, 128), i16),
        pltpu.VMEM((8, 128), f32),
        pltpu.VMEM((n_tp, rows // 2, 128), i16),
        pltpu.VMEM((n_tp, 8, 128), f32),
        pltpu.VMEM((n_tp, block, feats), f32),
        pltpu.VMEM((n_tp, block, 128), jnp.int32),
        pltpu.VMEM((n_tp, block, 128), f32),
        pltpu.SMEM((n_serve, cap), jnp.int32),
        pltpu.SMEM((wanted.shape[1],), jnp.int32),
        dma((4,)),
        dma((n_tp,)), dma((n_tp,)),
        dma((n_serve,)), dma((n_serve,)), dma((n_serve,)), dma((n_serve,)),
        dma((n_tp, n_tp)), dma((n_tp, n_tp)), dma((n_tp, n_tp)), dma((n_tp, n_tp)),
        dma((n_tp,)), dma((n_tp,)), dma((n_tp,)), dma((n_tp,)),
    ]
    return pl.pallas_call(
        functools.partial(kernel, (n_tp, n_serve, cap, held)),
        out_shape=jax.ShapeDtypeStruct((rows, feats), bf16),
        in_specs=[smem, smem, smem, hbm, hbm, hbm, hbm],
        out_specs=pl.BlockSpec(memory_space=pltpu.VMEM),
        scratch_shapes=scratch,
        compiler_params=pltpu.CompilerParams(
            collective_id=0, has_side_effects=True, vmem_limit_bytes=56 * 1024 * 1024
        ),
    )(home, wanted, tile_slot, hidden, kv_weight, panels, b_store)


def solution(mesh):
    in_specs = (
        P(("rep", "serve", "tp"), None),
        P("tp", None),
        P("serve", "tp", None),
        P("serve", None, "tp"),
        P("rep"),
        P("rep", None),
        P(("rep", "serve")),
    )
    out_specs = P(("rep", "serve"), "tp")
    return jax.shard_map(body, mesh=mesh, in_specs=in_specs, out_specs=out_specs, check_vma=False)
```

time: 229 us -> 86.7 us (0.38)
  waiting for transfers between devices: 128 us -> 0 us
  Pallas kernels: 0 us -> 84.8 us
  local copies, waits for them, and re-layouts: 26.4 us -> 1.77 us
  matrix products: 17 us -> 0 us
  blocking collectives: 16.9 us -> 0 us
  other arithmetic: 15.6 us -> 0 us
  between operations: 13.5 us -> 0.01 us
  starting transfers between devices: 10.6 us -> 0 us
    pallas_call x0 -> x1, Pallas kernels: none -> 84.8 us  [body(): pl.pallas_call(functools.partial(kernel, (n_tp, n_serve, cap, held)), out...]
    all_to_all x2 -> x0, waiting for transfers between devices: 66.4 us -> none  [the longest x1 46 us: body(): lax.all_to_all(send_shrink, 'serve', split_axis=0, concat_axis=0, tiled=T...]
    reduce_scatter x1 -> x0, waiting for transfers between devices: 60.1 us -> none  [body(): lax.psum_scatter(base_part, 'tp', scatter_dimension=1, tiled=True)]
    gather x8 -> x0, local copies, waits for them, and re-layouts: 23.4 us -> none  [the longest x1 6.64 us: body(): tile_shrink = jnp.take(shrink_panels, tile_slot, axis=0)]
    dot_general x3 -> x0, matrix products: 17 us -> none  [the longest x1 8.96 us: body(): base_part = jnp.dot(slices, kv_weight, preferred_element_type=jnp.float32)]
    all_to_all x1 -> x0, blocking collectives: 16.9 us -> none  [body(): lax.all_to_all(send_expand, 'serve', split_axis=0, concat_axis=0, tiled=T...]
    select_n x8 -> x0, other arithmetic: 12.4 us -> none  [the longest x1 4.69 us: body(): jnp.take(got_shrink.reshape((groups * slot_count,) + a_store.shape[1:]),...]
    all_to_all x2 -> x0, starting transfers between devices: 10.6 us -> none  [the longest x1 5.72 us: body(): lax.all_to_all(hidden, 'tp', split_axis=1, concat_axis=0, tiled=True)]
  transfers between devices with their start and end apart: 4 -> 0, of which waited for: 4 -> 0; matrix products, arithmetic and copies ran while one was open for 16% -> 0% of each run, Pallas kernels for 0% -> 0%
where the time goes in v1:
time: 86.7 us; the launch traced here: 86.5 us
  Pallas kernels  84.8 us (98%)
  local copies, waits for them, and re-layouts  1.77 us (2%)
    pallas_call x1, Pallas kernels, body(): pl.pallas_call(functools.partial(kernel, (n_tp, n_serve, cap, held)), out...  84.8 us
    unnamed x1, local copies, waits for them, and re-layouts  1.77 us

profile of v1, /device:TPU:0, one launch (start us, length us, event | category | flops | bytes accessed | tf_op | source)
XLA Modules:
  0.0 86.5 jit_solution(12198866491306155354)
XLA Ops:
  0.0 84.8 %shard_map.73 = bf16[384,512]{1,0:T(8,128)(2,1)} custom-call(s32[128]{0:T(128)} %home.1, s32[4,16]{1,0:T(4,128)} %wanted.1, s32[24]{0:T(128)} %tile_slot.1, bf16[96,8192]{1,0:T(8,128)(2,1)} %hidden.1, bf16[2048,2048]{1,0:T(8,128)(2,1)} %weight.1, bf16[32,64,2048]{2,1,0:T(8,128)(2,1)} %bitcast.1, bf16[32,64,512]{2,1,0:T(8,128)(2,1)} %b_store.1), custom_call_target="tpu_custom_call" | custom-call | tf_op jit(solution)/shard_map/pallas_call | solution.py:330
  84.8 1.8 %copy.9 = bf16[384,512]{1,0:T(8,128)(2,1)} copy(bf16[384,512]{1,0:T(8,128)(2,1)} %shard_map.73) | data formatting | bytes 786432

commit v2 on v1

--- a/solution.py
+++ b/solution.py
@@ -76,7 +76,7 @@
         )
 
     def part_copies(u, t):
-        c = flip(me, u, n_tp)
+        c = flip(me, u & -u, n_tp)
         return (
             pltpu.make_async_remote_copy(
                 src_ref=p_send.at[u, t], dst_ref=p_recv.at[u, t],
@@ -186,26 +186,50 @@
     load_x.wait()
     load_w.wait()
 
+    def product(t, u):
+        c = flip(me, u, n_tp)
+        return jnp.dot(
+            xs[t], w_vm[:, pl.ds(pl.multiple_of(c * feats, feats), feats)],
+            preferred_element_type=jnp.float32,
+        )
+
+    def send_part(u, t, part):
+        coded, scale = quantize(part)
+        p_send[u, t] = coded
+        p_scale_send[u, t] = scale
+        for copy in part_copies(u, t):
+            copy.start()
+
+    def with_received(u, t):
+        total = own[u // 2, t]
+        bit = 1
+        while bit < ((u & -u) or n_tp):
+            v, q = u | bit, t ^ bit
+            for copy in part_copies(v, q):
+                copy.wait_recv()
+            total = total + restore(p_recv[v, q], p_scale_recv[v, q, 0:1, 0:1])
+            bit *= 2
+        return total
+
+    def forward(bit, places_of):
+        for t in places_of:
+            for u in range(bit, n_tp, 2 * bit):
+                send_part(u, t, with_received(u, t))
+
     for t in range(n_tp):
-        j = flip(me, t, n_tp)
         if t:
             x_copy(t).wait_recv()
-        for u in range(1, n_tp):
-            c = flip(me, u, n_tp)
-            part = jnp.dot(
-                xs[t], w_vm[:, pl.ds(pl.multiple_of(c * feats, feats), feats)],
-                preferred_element_type=jnp.float32,
-            )
-            coded, scale = quantize(part)
-            p_send[u, t] = coded
-            p_scale_send[u, t] = scale
-            for copy in part_copies(u, t):
-                copy.start()
-
-        own[t] = jnp.dot(
-            xs[t], w_vm[:, pl.ds(pl.multiple_of(me * feats, feats), feats)],
-            preferred_element_type=jnp.float32,
-        )
+        for u in range(1, n_tp, 2):
+            send_part(u, t, product(t, u))
+        for u in range(0, n_tp, 2):
+            own[u // 2, t] = product(t, u)
+        if t >= 2 and t % 2 == 0:
+            forward(2, (t - 2, t - 1))
+    forward(2, (n_tp - 2, n_tp - 1))
+    bit = 4
+    while bit < n_tp:
+        forward(bit, range(n_tp))
+        bit *= 2
 
     lane = lax.broadcasted_iota(jnp.int32, (rows, 128), 1)
     lane_half = lane // rank
@@ -259,15 +283,11 @@
                     jnp.where(keep, piece, 0.0).astype(jnp.bfloat16), panel,
                     preferred_element_type=jnp.float32,
                 )
-    own[...] = own[...] + adapter_scale * update.reshape(n_tp, block, feats)
+    own[0] = own[0] + adapter_scale * update.reshape(n_tp, block, feats)
 
     for t in range(n_tp):
         j = flip(me, t, n_tp)
-        result = own[t]
-        for u in range(1, n_tp):
-            for copy in part_copies(u, u ^ t):
-                copy.wait_recv()
-            result = result + restore(p_recv[u, u ^ t], p_scale_recv[u, u ^ t, 0:1, 0:1])
+        result = with_received(0, t)
         out[pl.ds(pl.multiple_of(j * block, block), block), :] = result.astype(jnp.bfloat16)
 
     for u in range(1, n_tp):
@@ -316,7 +336,7 @@
         pltpu.VMEM((8, 128), f32),
         pltpu.VMEM((n_tp, rows // 2, 128), i16),
         pltpu.VMEM((n_tp, 8, 128), f32),
-        pltpu.VMEM((n_tp, block, feats), f32),
+        pltpu.VMEM((n_tp // 2, n_tp, block, feats), f32),
         pltpu.VMEM((n_tp, block, 128), jnp.int32),
         pltpu.VMEM((n_tp, block, 128), f32),
         pltpu.SMEM((n_serve, cap), jnp.int32),

time: 86.7 us -> 75.4 us (0.87)
  Pallas kernels: 84.8 us -> 73.5 us
    pallas_call x1, Pallas kernels: 84.8 us -> 73.5 us  [body(): pl.pallas_call(functools.partial(kernel, (n_tp, n_serve, cap, held)), out...]
where the time goes in v2:
time: 75.4 us; the launch traced here: 75.2 us
  Pallas kernels  73.5 us (97%)
  local copies, waits for them, and re-layouts  1.77 us (2%)
    pallas_call x1, Pallas kernels, body(): pl.pallas_call(functools.partial(kernel, (n_tp, n_serve, cap, held)), out...  73.5 us
    unnamed x1, local copies, waits for them, and re-layouts  1.77 us

profile of v2, /device:TPU:0, one launch (start us, length us, event | category | flops | bytes accessed | tf_op | source)
XLA Modules:
  0.0 75.2 jit_solution(8846265825754418044)
XLA Ops:
  0.0 73.5 %shard_map.73 = bf16[384,512]{1,0:T(8,128)(2,1)} custom-call(s32[128]{0:T(128)} %home.1, s32[4,16]{1,0:T(4,128)} %wanted.1, s32[24]{0:T(128)} %tile_slot.1, bf16[96,8192]{1,0:T(8,128)(2,1)} %hidden.1, bf16[2048,2048]{1,0:T(8,128)(2,1)} %weight.1, bf16[32,64,2048]{2,1,0:T(8,128)(2,1)} %bitcast.1, bf16[32,64,512]{2,1,0:T(8,128)(2,1)} %b_store.1), custom_call_target="tpu_custom_call" | custom-call | tf_op jit(solution)/shard_map/pallas_call | solution.py:350
  73.5 1.8 %copy.9 = bf16[384,512]{1,0:T(8,128)(2,1)} copy(bf16[384,512]{1,0:T(8,128)(2,1)} %shard_map.73) | data formatting | bytes 786432

commit v3 on v2

--- a/solution.py
+++ b/solution.py
@@ -113,8 +113,8 @@
     load_w = pltpu.make_async_copy(weight, w_vm, local_sem.at[3])
     load_a.start()
     load_x.start()
+    load_w.start()
     load_b.start()
-    load_w.start()
 
     barrier = pltpu.get_barrier_semaphore()
     for u in range(1, n_tp):
@@ -150,41 +150,45 @@
             send_a[u, i * rank:(i + 1) * rank, :] = a_vm[picks[u, i]]
         panel_copy(send_a, got_a, a_send, a_recv, u, u).start()
 
-    load_b.wait()
-
-    for u in range(n_serve - 1, 0, -1):
-        for i in range(cap):
-            send_b[u, i * rank:(i + 1) * rank, :] = b_vm[picks[u, i]]
-        panel_copy(send_b, got_b, bs_send, bs_recv, u, u).start()
-
     for i in range(cap):
         send_a[0, i * rank:(i + 1) * rank, :] = a_vm[picks[0, i]]
-        send_b[0, i * rank:(i + 1) * rank, :] = b_vm[picks[0, i]]
-
-    @pl.loop(0, need)
-    def _(e):
-        owner = home[wanted[group, e]] // held
-
-        def step(f, count):
-            same = (home[wanted[group, f]] // held) == owner
-            return count + jnp.where(jnp.logical_and(same, f < e), 1, 0)
-
-        earlier = lax.fori_loop(0, need, step, jnp.int32(0))
-        places[e] = flip(owner, group, n_serve) * cap + earlier
-
-    per_block = tiles // n_tp
-    for t in range(n_tp):
-        j = flip(me, t, n_tp)
-
-        @pl.loop(0, per_block)
-        def _(k):
-            place = places[tile_slot[j * per_block + k]]
-            row_slot[t, pl.ds(pl.multiple_of(k * tile_rows, tile_rows), tile_rows), :] = jnp.full(
-                (tile_rows, 128), place, jnp.int32
-            )
 
     load_x.wait()
     load_w.wait()
+
+    def place_rows():
+        load_b.wait()
+
+        for u in range(n_serve - 1, 0, -1):
+            for i in range(cap):
+                send_b[u, i * rank:(i + 1) * rank, :] = b_vm[picks[u, i]]
+            panel_copy(send_b, got_b, bs_send, bs_recv, u, u).start()
+
+        for i in range(cap):
+            send_b[0, i * rank:(i + 1) * rank, :] = b_vm[picks[0, i]]
+
+        @pl.loop(0, need)
+        def _(e):
+            owner = home[wanted[group, e]] // held
+
+            def step(f, count):
+                same = (home[wanted[group, f]] // held) == owner
+                return count + jnp.where(jnp.logical_and(same, f < e), 1, 0)
+
+            earlier = lax.fori_loop(0, need, step, jnp.int32(0))
+            places[e] = flip(owner, group, n_serve) * cap + earlier
+
+        per_block = tiles // n_tp
+        for t in range(n_tp):
+            j = flip(me, t, n_tp)
+
+            @pl.loop(0, per_block)
+            def _(k):
+                place = places[tile_slot[j * per_block + k]]
+                row_slot[t, pl.ds(pl.multiple_of(k * tile_rows, tile_rows), tile_rows), :] = jnp.full(
+                    (tile_rows, 128), place, jnp.int32
+                )
+
 
     def product(t, u):
         c = flip(me, u, n_tp)
@@ -223,6 +227,8 @@
             send_part(u, t, product(t, u))
         for u in range(0, n_tp, 2):
             own[u // 2, t] = product(t, u)
+        if t == 1:
+            place_rows()
         if t >= 2 and t % 2 == 0:
             forward(2, (t - 2, t - 1))
     forward(2, (n_tp - 2, n_tp - 1))

time: 75.4 us -> 75.4 us (level)
  no operation moved by 1% of the time
where the time goes in v3:
time: 75.4 us; the launch traced here: 75.2 us
  Pallas kernels  73.4 us (97%)
  local copies, waits for them, and re-layouts  1.77 us (2%)
    pallas_call x1, Pallas kernels, body(): pl.pallas_call(functools.partial(kernel, (n_tp, n_serve, cap, held)), out...  73.4 us
    unnamed x1, local copies, waits for them, and re-layouts  1.77 us

profile of v3, /device:TPU:0, one launch (start us, length us, event | category | flops | bytes accessed | tf_op | source)
XLA Modules:
  0.0 75.2 jit_solution(6855147109644712951)
XLA Ops:
  0.0 73.4 %shard_map.73 = bf16[384,512]{1,0:T(8,128)(2,1)} custom-call(s32[128]{0:T(128)} %home.1, s32[4,16]{1,0:T(4,128)} %wanted.1, s32[24]{0:T(128)} %tile_slot.1, bf16[96,8192]{1,0:T(8,128)(2,1)} %hidden.1, bf16[2048,2048]{1,0:T(8,128)(2,1)} %weight.1, bf16[32,64,2048]{2,1,0:T(8,128)(2,1)} %bitcast.1, bf16[32,64,512]{2,1,0:T(8,128)(2,1)} %b_store.1), custom_call_target="tpu_custom_call" | custom-call | tf_op jit(solution)/shard_map/pallas_call | solution.py:356
  73.5 1.8 %copy.9 = bf16[384,512]{1,0:T(8,128)(2,1)} copy(bf16[384,512]{1,0:T(8,128)(2,1)} %shard_map.73) | data formatting | bytes 786432

commit v4 on v3

--- a/solution.py
+++ b/solution.py
@@ -123,7 +123,7 @@
         pl.semaphore_signal(barrier, inc=1, device_id={"serve": flip(group, u, n_serve)})
     pl.semaphore_wait(barrier, n_tp - 1 + n_serve - 1)
 
-    for u in range(1, n_tp):
+    for u in range(n_tp - 1, 0, -1):
         x_copy(u).start()
 
     @pl.loop(0, n_serve)

time: 75.4 us -> 80.1 us (1.062)
  Pallas kernels: 73.4 us -> 78.2 us
    pallas_call x1, Pallas kernels: 73.4 us -> 78.2 us  [body(): pl.pallas_call(functools.partial(kernel, (n_tp, n_serve, cap, held)), out...]
where the time goes in v4:
time: 80.1 us; the launch traced here: 79.9 us
  Pallas kernels  78.2 us (98%)
  local copies, waits for them, and re-layouts  1.77 us (2%)
    pallas_call x1, Pallas kernels, body(): pl.pallas_call(functools.partial(kernel, (n_tp, n_serve, cap, held)), out...  78.2 us
    unnamed x1, local copies, waits for them, and re-layouts  1.77 us

profile of v4, /device:TPU:0, one launch (start us, length us, event | category | flops | bytes accessed | tf_op | source)
XLA Modules:
  0.0 79.9 jit_solution(15553915077537294591)
XLA Ops:
  0.0 78.2 %shard_map.73 = bf16[384,512]{1,0:T(8,128)(2,1)} custom-call(s32[128]{0:T(128)} %home.1, s32[4,16]{1,0:T(4,128)} %wanted.1, s32[24]{0:T(128)} %tile_slot.1, bf16[96,8192]{1,0:T(8,128)(2,1)} %hidden.1, bf16[2048,2048]{1,0:T(8,128)(2,1)} %weight.1, bf16[32,64,2048]{2,1,0:T(8,128)(2,1)} %bitcast.1, bf16[32,64,512]{2,1,0:T(8,128)(2,1)} %b_store.1), custom_call_target="tpu_custom_call" | custom-call | tf_op jit(solution)/shard_map/pallas_call | solution.py:356
  78.2 1.8 %copy.9 = bf16[384,512]{1,0:T(8,128)(2,1)} copy(bf16[384,512]{1,0:T(8,128)(2,1)} %shard_map.73) | data formatting | bytes 786432
